TPU v7x, 32 devices: a whole 2x2x4 slice. The times are simulated.
32 devices in a mesh: layer: 4 (over x, core), col: 8 (over z, y).
Axes of the slice: x: 2, y: 2, z: 4, core: 2. Of those that a mesh axis runs over, the one named last changes fastest.
Arguments:
- lower_panel: bfloat16 [4, 4096, 768], P('layer', 'col'), may hold values from -0.109375 to 0.109375
- upper_panel: bfloat16 [4, 768, 4096], P('layer', None, 'col'), may hold values from -6 to 6
- diag_inverse: bfloat16 [4, 1, 768, 768], P('layer'), may hold values from -1 to 2, as said below
- pivot_inverse: bfloat16 [2, 128, 128], replicated, may hold values from -0.1 to 0.1, as said below
- pattern: int32 [4, 2, 32], P('layer'), may hold values 0 or 1
- col_order: int32 [32], replicated, may hold values from 0 to 31, each once
- sep_blocks: int32 [2], replicated, may hold values from 0 to 31, as said below
Outputs:
- schur_top: bfloat16 [4096, 4096], P('layer', 'col')
Inputs may be any that keep to these rules, and one draw needn't show every extreme that they name: `diag_inverse`: each is the identity plus a full matrix of smaller entries. `pivot_inverse`: full matrices. `sep_blocks`: the 2 entries are distinct.
All inputs are finite; a program needn't handle non-finite values. No bound on the sum of `pattern` on one device may be relied on, other than what follows from the above.
Results may differ from a plain program's by a relative error of at most 0.0088.
Values may be sent and summed in bfloat16 or wider, within the bound.
A program may use at most 64 MiB of HBM per device.

v0:
```python
import jax
import jax.numpy as jnp
from jax import lax
from jax.sharding import PartitionSpec as P

NB = 128


def from_partner(value, axis, distance):
    mask = 2**distance
    pairs = [(source, source ^ mask) for source in range(lax.axis_size(axis))]
    return lax.ppermute(value, axis, pairs)


def broadcast(x, axis, root):
    mine = lax.axis_index(axis) == root
    return lax.psum(jnp.where(mine, x, jnp.zeros_like(x)), axis)


def share_rows(values, level):
    for bit in range(level + 1):
        other = from_partner(values, "layer", bit)
        values = (values.astype(jnp.float32) + other.astype(jnp.float32)).astype(jnp.bfloat16)
    return values


def shards(lower_panel, upper_panel, diag_inverse, pivot_inverse, pattern, col_order, sep_blocks):
    supernodes = diag_inverse.shape[1]
    node_width = diag_inverse.shape[2]
    local_cols = upper_panel.shape[2]
    col_index = lax.axis_index("col")
    first_col = col_index * local_cols
    nblocks = col_order.shape[0]
    solved = jnp.einsum(
        "sab,sbc->sac",
        diag_inverse[0],
        upper_panel[0].reshape(supernodes, node_width, local_cols),
        preferred_element_type=jnp.float32,
    )
    right = solved.astype(jnp.bfloat16).reshape(supernodes * node_width, local_cols)
    row_flags = jnp.repeat(pattern[0, 0], NB).astype(jnp.float32)
    all_col_flags = jnp.repeat(pattern[0, 1], NB).astype(jnp.float32)
    col_flags = lax.dynamic_slice_in_dim(all_col_flags, first_col, local_cols)
    product = jnp.dot(
        lax.all_gather(lower_panel[0], "col", axis=0, tiled=True),
        right,
        preferred_element_type=jnp.float32,
    )
    current = (-product * row_flags[:, None] * col_flags[None, :]).astype(jnp.bfloat16)
    layer_count = lax.axis_size("layer")
    layer_index = lax.axis_index("layer")
    levels = layer_count.bit_length() - 1
    positions = jnp.arange(nblocks, dtype=jnp.int32)
    total_rows = current.shape[0]
    span_rows = total_rows // layer_count
    col_blocks = (first_col + jnp.arange(local_cols, dtype=jnp.int32)) // NB
    held = current.reshape(layer_count, span_rows, local_cols)
    for level in range(levels):
        count = held.shape[0] // 2
        paired = held.reshape(count, 2, span_rows, local_cols)
        side = layer_index >> level & 1
        keep_half = lax.dynamic_index_in_dim(paired, side, 1, keepdims=False)
        send_half = lax.dynamic_index_in_dim(paired, 1 - side, 1, keepdims=False)
        partner = from_partner(send_half, "layer", level)
        total = keep_half.astype(jnp.float32) + partner.astype(jnp.float32)
        stride = 2 ** (level + 1)
        base = layer_index % stride
        span_ids = base + stride * jnp.arange(count, dtype=jnp.int32)
        global_rows = (
            span_ids[:, None] * span_rows + jnp.arange(span_rows, dtype=jnp.int32)[None, :]
        ).reshape(count * span_rows)
        separator = sep_blocks[level]
        position = jnp.sum(jnp.where(col_order == separator, positions, 0))
        owner = position * NB // local_cols
        offset = position * NB - owner * local_cols
        sep_row = separator * NB
        sep_span = sep_row // span_rows
        inner = sep_row - sep_span * span_rows
        holds = sep_span % stride == base
        local_span = jnp.where(holds, sep_span // stride, 0)
        zero = jnp.zeros((), jnp.int32)
        rows_here = lax.dynamic_slice(
            total, (local_span, inner, zero), (1, NB, local_cols)
        ).reshape(NB, local_cols)
        masked = jnp.where(holds, rows_here, jnp.zeros_like(rows_here)).astype(jnp.bfloat16)
        upper_rows = share_rows(masked, level)
        flat = total.reshape(count * span_rows, local_cols)
        local_panel = lax.dynamic_slice_in_dim(flat, offset, NB, 1).astype(jnp.bfloat16)
        local_factor = jnp.dot(
            local_panel, pivot_inverse[level], preferred_element_type=jnp.float32
        ).astype(jnp.bfloat16)
        factor = broadcast(local_factor, "col", owner)
        updated = flat - jnp.dot(factor, upper_rows, preferred_element_type=jnp.float32)
        keep = (global_rows // NB != separator)[:, None] & (col_blocks != position)[None, :]
        kept = jnp.where(keep, updated, jnp.zeros_like(updated)).astype(jnp.bfloat16)
        held = kept.reshape(count, span_rows, local_cols)
    result = held.reshape(span_rows, local_cols)
    return result


def solution(mesh):
    in_specs = (
        P("layer", "col", None),
        P("layer", None, "col"),
        P("layer", None, None, None),
        P(),
        P("layer", None, None),
        P(),
        P(),
    )
    out_specs = P("layer", "col")
    return jax.shard_map(shards, mesh=mesh, in_specs=in_specs, out_specs=out_specs, check_vma=False)
```

profile of v0, /device:TPU:25, one launch (start us, length us, event | category | flops | bytes accessed | tf_op | source)
XLA Modules:
  0.0 344.2 jit_solution(6543228791514767597)
XLA Ops:
  6.5 0.7 all-gather.3.cloned.1.call-update
  7.3 0.8 convert_bitcast_fusion.1
  8.2 1.9 convolution_convert_fusion.1
  10.1 97.7 %all-gather.3.cloned.1.call-done = bf16[1,4096,768]{2,1,0:T(8,128)(2,1)} async-done(((bf16[1,512,768]{2,1,0:T(8,128)(2,1)}), bf16[1,4096,768]{2,1,0:T(8,128)(2,1)}) %all-gather.3.cloned.1.call-update) | async-done | bytes 6291472 | tf_op jit(solution)/shard_map/all_gather | solution.py:45
  107.9 8.5 %fusion.1 = bf16[4096,512]{0,1:T(8,128)(2,1)} fusion(bf16[768,512]{1,0:T(8,128)(2,1)S(1)} %convolution_convert_fusion.1, bf16[1,4096,768]{2,1,0:T(8,128)(2,1)} %all-gather.3.cloned.1.call-done, f32[512]{0:T(512)S(1)} %dynamic_slice.30, f32[4096]{0:T(1024)S(1)} %get-tuple-element.14), kind=kOutput, calls=%fused_computation.2 | convolution fusion | flops 3229614080 | bytes 11290624 | tf_op jit(solution)/shard_map/dot_general | solution.py:44
  116.4 7.8 %reshape_reshape.6 = bf16[2,2,1024,512]{2,1,0,3:T(2,128)(2,1)} reshape(bf16[4096,512]{0,1:T(8,128)(2,1)} %fusion.1) | data formatting | bytes 8388608 | tf_op jit(solution)/shard_map/reshape;reshape | solution.py:60
  124.2 11.3 %constant_dynamic-slice_fusion.1 = (bf16[2,1,1024,512]{2,1,0,3:T(2,128)(2,1)}, bf16[2,1,1024,512]{2,1,0,3:T(2,128)(2,1)}) fusion(bf16[2,2,1024,512]{2,1,0,3:T(2,128)(2,1)} %reshape_reshape.6, s32[]{:T(128)S(6)} %select_n.159, s32[]{:T(128)S(6)} %select_n.160), kind=kLoop, calls=%fused_computation.66 | loop fusion | bytes 8388616 | tf_op jit(solution)/shard_map/jit(dynamic_index_in_dim)/dynamic_slice | solution.py:62
  135.5 10.5 %copy.9 = bf16[2,1,1024,512]{3,2,0,1:T(8,128)(2,1)} copy(bf16[2,1,1024,512]{2,1,0,3:T(2,128)(2,1)} %get-tuple-element.8) | data formatting | bytes 4194304 | tf_op jit(solution)/shard_map/jit(dynamic_index_in_dim)/dynamic_slice | solution.py:63
  146.0 0.5 collective-permute-start
  146.5 0.6 fusion.34
  147.1 1.9 fusion.32
  149.6 9.0 %copy.10 = bf16[2,1,1024,512]{3,2,0,1:T(8,128)(2,1)S(1)} copy(bf16[2,1,1024,512]{2,1,0,3:T(2,128)(2,1)} %get-tuple-element.7) | data formatting | bytes 4194304
  158.6 2.2 convert_add_fusion
  160.9 1.9 copy-done.1
  162.8 1.1 fusion.4
  164.8 1.0 fusion.12
  165.8 0.6 fusion.20
  166.5 0.6 broadcast_compare_fusion
  167.0 0.1 collective-permute-done.1
  167.2 66.0 %all-reduce.3.cloned.1.call-done = bf16[2048,128]{1,0:T(8,128)(2,1)} async-done(((bf16[2048,128]{1,0:T(8,128)(2,1)}), bf16[2048,128]{1,0:T(8,128)(2,1)}) %all-reduce.3.cloned.1.call-update) | async-done | bytes 524304 | tf_op jit(solution)/shard_map/psum | solution.py:17
  233.2 3.1 select_convert_fusion
  236.3 1.3 copy-done.2
  237.7 1.2 collective-permute-start.2
  240.1 19.9 %collective-permute-done.2 = bf16[1,1024,512]{2,1,0:T(8,128)(2,1)} collective-permute-done((bf16[1,1024,512]{2,1,0:T(8,128)(2,1)S(1)}, bf16[1,1024,512]{2,1,0:T(8,128)(2,1)}, u32[]{:S(2)}, u32[]{:S(2)}) %collective-permute-start.2) | collective-permute-done | bytes 1048608 | tf_op jit(solution)/shard_map/ppermute | solution.py:12
  260.0 1.8 convert_add_fusion.1
  261.9 3.5 %collective-permute-start.3 = (bf16[128,512]{1,0:T(8,128)(2,1)S(1)}, bf16[128,512]{1,0:T(8,128)(2,1)S(1)}, u32[]{:S(2)}, u32[]{:S(2)}) collective-permute-start(bf16[128,512]{1,0:T(8,128)(2,1)S(1)} %fusion.13), channel_id=1, source_target_pairs={{0,8},{8,0},{16,24},{24,16},{1,9},{9,1},{17,25},{25,17},{2,10},{10... | collective-permute-start | bytes 393224 | tf_op jit(solution)/shard_map/ppermute | solution.py:12
  265.4 1.7 fusion.8
  267.2 1.2 collective-permute-start.4
  268.3 0.6 broadcast_compare_fusion.1
  268.9 0.6 fusion.24
  269.5 65.7 %all-reduce.5.cloned.1.call-done = bf16[1024,128]{1,0:T(8,128)(2,1)} async-done(((bf16[1024,128]{1,0:T(8,128)(2,1)}), bf16[1024,128]{1,0:T(8,128)(2,1)}) %all-reduce.5.cloned.1.call-update) | async-done | bytes 262160 | tf_op jit(solution)/shard_map/psum | solution.py:17
  335.2 2.4 fusion.6
  (26 shorter events, 0.6 us)
Async XLA Ops:
  6.5 1.7 copy-start
  6.5 101.3 %all-gather.3.cloned.1.call-start = ((), (), s32[]{:S(2)}) async-start(), calls=%async_computation.2 | async-start | bytes 7077888 | tf_op jit(solution)/shard_map/all_gather | solution.py:45
  7.3 225.9 %all-reduce.3.cloned.1.call-start = ((), (), s32[]{:S(2)}) async-start(), calls=%async_computation | async-start | bytes 1048576 | tf_op jit(solution)/shard_map/psum | solution.py:17
  135.5 11.0 %copy-start.4 = (s32[2]{0:T(128)S(1)}, s32[2]{0:T(128)}, u32[]{:S(2)}) copy-start(s32[2]{0:T(128)} %param.13) | copy-start | bytes 28
  135.5 11.7 %copy-start.5 = (s32[32]{0:T(128)S(1)}, s32[32]{0:T(128)}, u32[]{:S(2)}) copy-start(s32[32]{0:T(128)} %param.12) | copy-start | bytes 388
  146.0 12.7 %collective-permute-start = (bf16[2,1024,512]{2,1,0:T(8,128)(2,1)}, bf16[2,1024,512]{2,1,0:T(8,128)(2,1)}, u32[]{:S(2)}, u32[]{:S(2)}) collective-permute-start(bf16[2,1024,512]{2,1,0:T(8,128)(2,1)} %bitcast.11), channel_id=1, source_target_pairs={{0,8},{8,0},{16,24},{24,16},{1,9},{9,1},{17,25},{25,17},{2,10},{10... | collective-permute-start | bytes 6291464 | tf_op jit(solution)/shard_map/ppermute | solution.py:12
  158.6 4.2 %copy-start.3 = (bf16[2,128,128]{2,1,0:T(8,128)(2,1)S(1)}, bf16[2,128,128]{2,1,0:T(8,128)(2,1)}, u32[]{:S(2)}) copy-start(bf16[2,128,128]{2,1,0:T(8,128)(2,1)} %param.10) | copy-start | bytes 196612
  160.9 1.9 copy-start.1
  163.9 171.3 %all-reduce.5.cloned.1.call-start = ((), (), s32[]{:S(2)}) async-start(), calls=%async_computation.1 | async-start | bytes 524288 | tf_op jit(solution)/shard_map/psum | solution.py:17
  165.7 1.4 collective-permute-start.1
  236.3 1.3 copy-start.2
  237.7 22.3 %collective-permute-start.2 = (bf16[1,1024,512]{2,1,0:T(8,128)(2,1)S(1)}, bf16[1,1024,512]{2,1,0:T(8,128)(2,1)}, u32[]{:S(2)}, u32[]{:S(2)}) collective-permute-start(bf16[1,1024,512]{2,1,0:T(8,128)(2,1)S(1)} %dynamic-slice_bitcast_fusion), channel_id=1, source_target_pairs={{0,16},{8,24},{16,0},{24,8},{1,17},{9,25},{17,1},{25,9},{2,18},{10... | collective-permute-start | bytes 3145736 | tf_op jit(solution)/shard_map/ppermute | solution.py:12
  261.9 5.2 %collective-permute-start.3 = (bf16[128,512]{1,0:T(8,128)(2,1)S(1)}, bf16[128,512]{1,0:T(8,128)(2,1)S(1)}, u32[]{:S(2)}, u32[]{:S(2)}) collective-permute-start(bf16[128,512]{1,0:T(8,128)(2,1)S(1)} %fusion.13), channel_id=1, source_target_pairs={{0,8},{8,0},{16,24},{24,16},{1,9},{9,1},{17,25},{25,17},{2,10},{10... | collective-permute-start | bytes 393224 | tf_op jit(solution)/shard_map/ppermute | solution.py:12
  267.2 68.1 %collective-permute-start.4 = (bf16[128,512]{1,0:T(8,128)(2,1)S(1)}, bf16[128,512]{1,0:T(8,128)(2,1)S(1)}, u32[]{:S(2)}, u32[]{:S(2)}) collective-permute-start(bf16[128,512]{1,0:T(8,128)(2,1)S(1)} %add_convert_fusion.1), channel_id=1, source_target_pairs={{0,16},{8,24},{16,0},{24,8},{1,17},{9,25},{17,1},{25,9},{2,18},{10... | collective-permute-start | bytes 393224 | tf_op jit(solution)/shard_map/ppermute | solution.py:12
Sparse Core Ops, SparseCore 0:
  9.5 98.2 all-gather.2
  164.1 69.0 all-reduce.2
  267.2 67.9 all-reduce.4
where the time goes:
time: 350 us; the launch traced here: 344 us
  waiting for transfers between devices  250 us (71%)
  local copies, waits for them, and re-layouts  42.7 us (12%)
  matrix products  18.7 us (5%)
  between operations  15.8 us (5%)
  other arithmetic  10.2 us (3%)
  starting transfers between devices  6.49 us (2%)
    psum x2, waiting for transfers between devices, broadcast(): return lax.psum(jnp.where(mine, x, jnp.zeros_like(x)), axis)  132 us
    all_gather x1, waiting for transfers between devices, shards(): lax.all_gather(lower_panel[0], 'col', axis=0, tiled=True)  97.7 us
    ppermute x5, waiting for transfers between devices, from_partner(): return lax.ppermute(value, axis, pairs)  20 us
    unnamed x13, local copies, waits for them, and re-layouts  12.3 us
    dynamic_slice x1, local copies, waits for them, and re-layouts, shards(): keep_half = lax.dynamic_index_in_dim(paired, side, 1, keepdims=False)  11.3 us
    dynamic_slice x1, local copies, waits for them, and re-layouts, shards(): send_half = lax.dynamic_index_in_dim(paired, 1 - side, 1, keepdims=False)  10.5 us
    dot_general x1, matrix products, shards(): jnp.dot(lax.all_gather(lower_panel[0], 'col', axis=0, tiled=True), right,...  8.48 us
    another operation x1, local copies, waits for them, and re-layouts, shards(): paired = held.reshape(count, 2, span_rows, local_cols)  7.83 us
  transfers between devices with their start and end apart: 8, of which 5 were waited for; matrix products, arithmetic and copies ran while one was open for 6% of the time, Pallas kernels for 0%

commit v1 on v0

--- a/solution.py
+++ b/solution.py
@@ -1,9 +1,395 @@
+import functools
+
 import jax
 import jax.numpy as jnp
 from jax import lax
+from jax.experimental import pallas as pl
+from jax.experimental.pallas import tpu as pltpu
 from jax.sharding import PartitionSpec as P
 
 NB = 128
+F32 = jnp.float32
+BF16 = jnp.bfloat16
+MESH = pl.DeviceIdType.MESH
+
+
+def dot(a, b):
+    return jnp.dot(a, b, preferred_element_type=F32)
+
+
+def fused_kernel(
+    col_count, l_ref, u_ref, d_ref, piv_ref, v0, flag_ref, keep_ref, pat_ref, hot_ref, out_ref,
+    lbuf, rbuf, pbuf, cin, xin, vy, vr, vl, vsr, vsl, s_acc, s_own, s_core, s_tot, s_x,
+    y_send, yv_send, zr_send, zl_send, vr_send, vl_send, l_recv, vy_recv, vr_recv, vl_recv,
+    c_send, c_recv, x_send, x_recv, s_send, s_recv,
+):
+    piece_rows, width = l_ref.shape
+    cols = u_ref.shape[1]
+    ext = rbuf.shape[1]
+    nz = col_count // 2
+    per_piece = piece_rows // NB
+    layer = lax.axis_index("layer")
+    core, xx = layer % 2, layer // 2
+    ci = lax.axis_index("col")
+    y, z = ci % 2, ci // 2
+    core_peer = {"layer": layer + 1 - 2 * core}
+    x_peer = {"layer": layer + 2 - 4 * xx}
+    y_peer = {"col": ci + 1 - 2 * y}
+    right, left = {"col": ci + 2}, {"col": ci - 2}
+    has_right, has_left = z < nz - 1, z > 0
+
+    def copy(src, dst, send, recv, peer):
+        return pltpu.make_async_remote_copy(
+            src_ref=src, dst_ref=dst, send_sem=send, recv_sem=recv, device_id=peer, device_id_type=MESH
+        )
+
+    def piece(p):
+        return pl.ds(pl.multiple_of(p * piece_rows, piece_rows), piece_rows)
+
+    barrier = pltpu.get_barrier_semaphore()
+    for peer in (core_peer, x_peer, y_peer):
+        pl.semaphore_signal(barrier, inc=1, device_id=peer, device_id_type=MESH)
+
+    @pl.when(has_right)
+    def _():
+        pl.semaphore_signal(barrier, inc=1, device_id=right, device_id_type=MESH)
+
+    @pl.when(has_left)
+    def _():
+        pl.semaphore_signal(barrier, inc=1, device_id=left, device_id_type=MESH)
+
+    pl.semaphore_wait(barrier, 3 + jnp.where(has_right, 1, 0) + jnp.where(has_left, 1, 0))
+
+    parts = v0.shape[0] // (2 * NB)
+
+    def vpart(k):
+        return pl.ds(k * 2 * NB, 2 * NB)
+
+    def v_y(k):
+        return copy(v0.at[vpart(k)], vy.at[vpart(k)], yv_send.at[k], vy_recv.at[k], y_peer)
+
+    def v_right(k):
+        return copy(vsr.at[vpart(k)], vr.at[vpart(k)], vr_send.at[k], vr_recv.at[k], right)
+
+    def v_left(k):
+        return copy(vsl.at[vpart(k)], vl.at[vpart(k)], vl_send.at[k], vl_recv.at[k], left)
+
+    for k in range(parts):
+        v_y(k).start()
+
+    lbuf[piece(ci), :] = l_ref[...]
+
+    def z_right(p):
+        return copy(lbuf.at[piece(p)], lbuf.at[piece(p)], zr_send.at[p // 2], l_recv.at[p], right)
+
+    def z_left(p):
+        return copy(lbuf.at[piece(p)], lbuf.at[piece(p)], zl_send.at[p // 2], l_recv.at[p], left)
+
+    def over_y(p):
+        return copy(lbuf.at[piece(p)], lbuf.at[piece(p)], y_send.at[p // 2], l_recv.at[p], y_peer)
+
+    @pl.when(has_right)
+    def _():
+        z_right(ci).start()
+
+    @pl.when(has_left)
+    def _():
+        z_left(ci).start()
+
+    over_y(ci).start()
+
+    supers, node = d_ref.shape[0], d_ref.shape[1]
+    for s in range(supers):
+        solved = dot(d_ref[s], u_ref[s * node : (s + 1) * node, :])
+        rounded = solved.astype(BF16).astype(F32)
+        rbuf[s * node : (s + 1) * node, 0:cols] = (rounded * flag_ref[:, 0:cols]).astype(BF16)
+
+    for k in range(parts):
+        rows = vpart(k)
+        v_y(k).wait_recv()
+        v0_sum = v0[rows, :] + vy[rows, :]
+        vsr[rows, :] = v0_sum
+        vsl[rows, :] = v0_sum
+
+        def go_right(k=k, rows=rows):
+            @pl.when(has_left)
+            def _():
+                v_right(k).wait_recv()
+                vsr[rows, :] = vsr[rows, :] + vr[rows, :]
+
+            @pl.when(has_right)
+            def _():
+                v_right(k).start()
+
+        def go_left(k=k, rows=rows):
+            @pl.when(has_right)
+            def _():
+                v_left(k).wait_recv()
+                vsl[rows, :] = vsl[rows, :] + vl[rows, :]
+
+            @pl.when(has_left)
+            def _():
+                v_left(k).start()
+
+        pl.when(z < nz // 2)(go_right)
+        pl.when(z >= nz // 2)(go_left)
+
+    for k in range(parts):
+        rows = vpart(k)
+
+        def go_right(k=k, rows=rows):
+            v_right(k).wait_recv()
+            vsr[rows, :] = vsr[rows, :] + vr[rows, :]
+
+            @pl.when(has_right)
+            def _():
+                v_right(k).start()
+
+        def go_left(k=k, rows=rows):
+            v_left(k).wait_recv()
+            vsl[rows, :] = vsl[rows, :] + vl[rows, :]
+
+            @pl.when(has_left)
+            def _():
+                v_left(k).start()
+
+        pl.when(z < nz // 2)(go_left)
+        pl.when(z >= nz // 2)(go_right)
+
+    vall = vsr[...] + vsl[...] - (v0[...] + vy[...])
+    for s in range(supers):
+        solved = dot(d_ref[s], vall[s * node : (s + 1) * node, :])
+        rounded = solved.astype(BF16).astype(F32)
+        rbuf[s * node : (s + 1) * node, cols:ext] = (rounded * flag_ref[:, cols:ext]).astype(BF16)
+
+    s_acc[...] = jnp.zeros_like(s_acc)
+    per_span = col_count // 4
+
+    def slot_of(p):
+        return (p // per_span // 2) * per_span + p % per_span
+
+    def to_core(p):
+        return copy(pbuf.at[piece(p)], cin.at[slot_of(p)], c_send.at[slot_of(p)], c_recv.at[slot_of(p)], core_peer)
+
+    def to_x(p):
+        return copy(pbuf.at[piece(p)], xin.at[p % per_span], x_send.at[p % per_span], x_recv.at[p % per_span], x_peer)
+
+    def process(p):
+        rows = lbuf[piece(p), :]
+        for n in range(0, ext, 2 * NB):
+            acc = dot(rows, rbuf[:, n : n + 2 * NB])
+            found = [None, None]
+            for j in range(per_piece):
+                block = p * per_piece + j
+                flagged = acc[j * NB : (j + 1) * NB] * pat_ref[0, block].astype(F32)
+                pbuf[pl.ds(pl.multiple_of(block * NB, NB), NB), n : n + 2 * NB] = flagged.astype(BF16)
+                for k in range(2):
+                    term = flagged * hot_ref[k, block]
+                    found[k] = term if j == 0 else found[k] + term
+            for k in range(2):
+                s_acc[k * NB : (k + 1) * NB, n : n + 2 * NB] += found[k]
+        span = p // per_span
+
+        @pl.when(span % 2 != core)
+        def _():
+            to_core(p).start()
+
+        @pl.when(span % 2 == core)
+        def _():
+            to_core(p).wait_recv()
+            slot = slot_of(p)
+
+            @pl.loop(0, per_piece)
+            def _(j):
+                at = pl.ds(pl.multiple_of(p * piece_rows + j * NB, NB), NB)
+                here = pl.ds(pl.multiple_of(j * NB, NB), NB)
+                pbuf[at, :] = (pbuf[at, :].astype(F32) + cin[slot, here, :].astype(F32)).astype(BF16)
+
+            @pl.when(span // 2 != xx)
+            def _():
+                to_x(p).start()
+
+    def place(i):
+        dist = (i + 1) // 2
+        return z + dist * (1 - 2 * (i % 2))
+
+    events = 2 * nz - 1
+
+    @pl.loop(0, events + 2)
+    def _(i):
+        zc = place(i)
+
+        @pl.when((i < events) & (zc >= 0) & (zc < nz))
+        def _():
+            p = zc * 2 + y
+
+            @pl.when(i > 0)
+            def _():
+                over_y(p).wait_recv()
+
+                @pl.when(has_right & (zc < z))
+                def _():
+                    z_right(p).start()
+
+                @pl.when(has_left & (zc > z))
+                def _():
+                    z_left(p).start()
+
+                over_y(p).start()
+
+            process(p)
+
+        zo = place(jnp.maximum(i - 2, 0))
+
+        @pl.when((i >= 2) & (zo >= 0) & (zo < nz))
+        def _():
+            p = zo * 2 + 1 - y
+            over_y(p).wait_recv()
+            process(p)
+
+    def s_copy(src, dst, k, peer):
+        return copy(src, dst, s_send.at[k], s_recv.at[k], peer)
+
+    s_own[...] = s_acc[...].astype(BF16)
+    swap = s_copy(s_own, s_core, 0, core_peer)
+    swap.start()
+    swap.wait()
+    s_tot[...] = (s_own[...].astype(F32) + s_core[...].astype(F32)).astype(BF16)
+    mine = pl.ds(pl.multiple_of(core * NB, NB), NB)
+    over_x = s_copy(s_tot.at[mine], s_x.at[mine], 1, x_peer)
+    over_x.start()
+    over_x.wait_recv()
+    share = s_copy(s_x.at[mine], s_x.at[mine], 2, core_peer)
+    share.start()
+    share.wait_recv()
+
+    pos_col = [cols, cols + NB]
+    upper = jnp.concatenate([s_tot[0:NB, 0:cols], s_x[0:NB, 0:cols]], axis=0)
+    upper_p = jnp.concatenate([s_tot[0:NB, pos_col[1] : ext], s_x[0:NB, pos_col[1] : ext]], axis=0)
+    keep_c = [keep_ref[k : k + 1, :] for k in range(2)]
+
+    def factors(a, b):
+        return jnp.concatenate([dot(a, piv_ref[0]).astype(BF16), dot(b, piv_ref[0]).astype(BF16)], axis=1)
+
+    fs = factors(s_tot[NB : 2 * NB, cols : cols + NB], s_x[NB : 2 * NB, cols : cols + NB])
+    last = s_tot[NB : 2 * NB, 0:cols].astype(F32) + s_x[NB : 2 * NB, 0:cols].astype(F32)
+    upper2 = ((last - dot(fs, upper)) * keep_c[0]).astype(BF16)
+
+    for q in range(per_span):
+        p = layer * per_span + q
+
+        to_x(p).wait_recv()
+        at = piece(p)
+        f0 = factors(pbuf[at, cols : cols + NB], xin[q, :, cols : cols + NB])
+
+        def keep_rows(value, k):
+            kept = [
+                value[j * NB : (j + 1) * NB] * (1.0 - hot_ref[k, p * per_piece + j]) for j in range(per_piece)
+            ]
+            return jnp.concatenate(kept, axis=0)
+
+        panel = pbuf[at, pos_col[1] : ext].astype(F32) + xin[q, :, pos_col[1] : ext].astype(F32)
+        panel = keep_rows(panel - dot(f0, upper_p), 0).astype(BF16)
+        f2 = dot(panel, piv_ref[1]).astype(BF16)
+        total = pbuf[at, 0:cols].astype(F32) + xin[q, :, 0:cols].astype(F32)
+        total = keep_rows(total - dot(f0, upper), 0) * keep_c[0]
+        final = keep_rows(total - dot(f2, upper2), 1) * keep_c[1]
+        out_ref[q * piece_rows : (q + 1) * piece_rows, :] = final.astype(BF16)
+
+    over_x.wait_send()
+    share.wait_send()
+    for k in range(parts):
+        v_y(k).wait_send()
+
+        @pl.when(has_right)
+        def _():
+            v_right(k).wait_send()
+
+        @pl.when(has_left)
+        def _():
+            v_left(k).wait_send()
+
+    @pl.loop(0, nz)
+    def _(zc):
+        p = zc * 2 + y
+        over_y(p).wait_send()
+
+        @pl.when(has_right & (zc <= z))
+        def _():
+            z_right(p).wait_send()
+
+        @pl.when(has_left & (zc >= z))
+        def _():
+            z_left(p).wait_send()
+
+    @pl.loop(0, col_count)
+    def _(p):
+        span = p // per_span
+
+        @pl.when(span % 2 != core)
+        def _():
+            to_core(p).wait_send()
+
+        @pl.when((span % 2 == core) & (span // 2 != xx))
+        def _():
+            to_x(p).wait_send()
+
+
+def fused(lower_panel, upper_panel, diag_inverse, pivot_inverse, pattern, col_order, sep_blocks):
+    col_count = lax.axis_size("col")
+    piece_rows, width = lower_panel.shape[1:]
+    cols = upper_panel.shape[2]
+    ext = cols + 2 * NB
+    nz, slots = col_count // 2, col_count // 2
+    total_rows = piece_rows * col_count
+    per_span = col_count // 4
+    parts = width // (2 * NB)
+    positions = jnp.arange(col_order.shape[0], dtype=jnp.int32)
+    pos = jnp.sum(jnp.where(col_order[None, :] == sep_blocks[:, None], positions[None, :], 0), axis=1)
+    blocks = cols // NB
+    first = lax.axis_index("col") * blocks
+    masked = []
+    for k in range(2):
+        local = pos[k] - first
+        inside = (local >= 0) & (local < blocks)
+        taken = lax.dynamic_slice_in_dim(upper_panel[0], jnp.clip(local, 0, blocks - 1) * NB, NB, 1)
+        masked.append(jnp.where(inside, taken, jnp.zeros_like(taken)))
+    masked = jnp.concatenate(masked, axis=1)
+    own_flags = lax.dynamic_slice_in_dim(pattern[0, 1], first, blocks)
+    flags = -jnp.repeat(jnp.concatenate([own_flags, pattern[0, 1][pos]]), NB)[None, :].astype(F32)
+    col_block = first + jnp.arange(cols, dtype=jnp.int32) // NB
+    keep = (col_block[None, :] != pos[:, None]).astype(F32)
+    hot = (positions[None, :] == sep_blocks[:, None]).astype(F32)
+    vmem = pl.BlockSpec(memory_space=pltpu.VMEM)
+    smem = pl.BlockSpec(memory_space=pltpu.SMEM)
+    dma = pltpu.SemaphoreType.DMA
+    v_shape = pltpu.VMEM((width, 2 * NB), BF16)
+    s_shape = pltpu.VMEM((2 * NB, ext), BF16)
+    return pl.pallas_call(
+        functools.partial(fused_kernel, col_count),
+        out_shape=jax.ShapeDtypeStruct((per_span * piece_rows, cols), BF16),
+        in_specs=[vmem] * 7 + [smem] * 2,
+        out_specs=vmem,
+        scratch_shapes=[
+            pltpu.VMEM((total_rows, width), BF16),
+            pltpu.VMEM((width, ext), BF16),
+            pltpu.VMEM((total_rows, ext), BF16),
+            pltpu.VMEM((slots, piece_rows, ext), BF16),
+            pltpu.VMEM((per_span, piece_rows, ext), BF16),
+            v_shape, v_shape, v_shape, v_shape, v_shape,
+            pltpu.VMEM((2 * NB, ext), F32), s_shape, s_shape, s_shape, s_shape,
+            dma((nz,)), dma((parts,)), dma((nz,)), dma((nz,)), dma((parts,)), dma((parts,)),
+            dma((col_count,)), dma((parts,)), dma((parts,)), dma((parts,)),
+            dma((slots,)), dma((slots,)), dma((per_span,)), dma((per_span,)), dma((3,)), dma((3,)),
+        ],
+        compiler_params=pltpu.CompilerParams(
+            collective_id=0, has_side_effects=True, vmem_limit_bytes=56 * 2**20
+        ),
+        cost_estimate=pl.CostEstimate(flops=6 * 10**9, bytes_accessed=5 * 10**6, transcendentals=0),
+    )(
+        lower_panel[0], upper_panel[0], diag_inverse[0], pivot_inverse, masked, flags, keep,
+        pattern[0], hot,
+    )
 
 
 def from_partner(value, axis, distance):
@@ -98,6 +484,21 @@
     return result
 
 
+def fits(mesh, args):
+    layers, columns = mesh.shape["layer"], mesh.shape["col"]
+    lower_panel, upper_panel, diag_inverse = args[:3]
+    rows, width = lower_panel.shape[1] // columns, lower_panel.shape[2]
+    cols = upper_panel.shape[2] // columns
+    return (
+        layers == 4
+        and columns % layers == 0
+        and rows % NB == 0
+        and cols % (2 * NB) == 0
+        and width % (2 * NB) == 0
+        and diag_inverse.shape[2] % NB == 0
+    )
+
+
 def solution(mesh):
     in_specs = (
         P("layer", "col", None),
@@ -109,4 +510,9 @@
         P(),
     )
     out_specs = P("layer", "col")
-    return jax.shard_map(shards, mesh=mesh, in_specs=in_specs, out_specs=out_specs, check_vma=False)
+
+    def run(*args):
+        body = fused if fits(mesh, args) else shards
+        return jax.shard_map(body, mesh=mesh, in_specs=in_specs, out_specs=out_specs, check_vma=False)(*args)
+
+    return run

time: 350 us -> 131 us (0.37); the launches traced: 344 us -> 131 us
  waiting for transfers between devices: 250 us -> 0 us
  Pallas kernels: 0 us -> 120 us
  local copies, waits for them, and re-layouts: 42.7 us -> 4.89 us
  matrix products: 18.7 us -> 0 us
  between operations: 15.8 us -> 1.26 us
  starting transfers between devices: 6.49 us -> 0 us
  other arithmetic: 10.2 us -> 4.8 us
    psum x2 -> x0, waiting for transfers between devices: 132 us -> none  [broadcast(): return lax.psum(jnp.where(mine, x, jnp.zeros_like(x)), axis)]
    pallas_call x0 -> x1, Pallas kernels: none -> 120 us  [fused(): pl.pallas_call(functools.partial(fused_kernel, col_count), out_shape=jax....]
    all_gather x1 -> x0, waiting for transfers between devices: 97.7 us -> none  [shards(): lax.all_gather(lower_panel[0], 'col', axis=0, tiled=True)]
    dynamic_slice x3 -> x1, local copies, waits for them, and re-layouts: 21.9 us -> 0.07 us  [fused(): own_flags = lax.dynamic_slice_in_dim(pattern[0, 1], first, blocks)]
    ppermute x5 -> x0, waiting for transfers between devices: 20 us -> none  [from_partner(): return lax.ppermute(value, axis, pairs)]
    dot_general x6 -> x0, matrix products: 18.7 us -> none  [the longest x1 8.48 us: shards(): jnp.dot(lax.all_gather(lower_panel[0], 'col', axis=0, tiled=True), right,...]
    unnamed x13 -> x3, local copies, waits for them, and re-layouts: 12.3 us -> 2.92 us
    another operation x1 -> x0, local copies, waits for them, and re-layouts: 7.83 us -> none  [shards(): paired = held.reshape(count, 2, span_rows, local_cols)]
  transfers between devices with their start and end apart: 8 -> 0, of which waited for: 5 -> 0; matrix products, arithmetic and copies ran while one was open for 6% -> 0% of each run, Pallas kernels for 0% -> 0%
where the time goes in v1:
time: 131 us
  Pallas kernels  120 us (92%)
  local copies, waits for them, and re-layouts  4.89 us (4%)
  other arithmetic  4.8 us (4%)
    pallas_call x1, Pallas kernels, fused(): pl.pallas_call(functools.partial(fused_kernel, col_count), out_shape=jax....  120 us
    unnamed x3, local copies, waits for them, and re-layouts  2.92 us

profile of v1, /device:TPU:25, one launch (start us, length us, event | category | flops | bytes accessed | tf_op | source)
XLA Modules:
  0.0 130.6 jit_solution(6519007729907545635)
XLA Ops:
  0.0 0.9 fusion.4
  0.9 1.3 compare_convert_fusion.1.hot_ref
  2.2 0.6 fusion.9
  4.0 0.7 fusion.8
  4.7 0.1 fusion.5
  4.7 0.7 compare_convert_fusion.keep_ref
  5.4 0.6 gather_fusion
  6.0 0.1 fusion.7
  6.1 0.1 broadcast_bitcast_fusion
  6.2 0.6 copy.10
  6.8 1.1 select_bitcast_fusion.1
  7.9 0.8 pad_maximum_fusion.v0
  8.7 119.7 %shard_map.73 = bf16[1024,512]{1,0:T(8,128)(2,1)} custom-call(bf16[512,768]{1,0:T(8,128)(2,1)} %bitcast.27, bf16[768,512]{1,0:T(8,128)(2,1)} %bitcast.24, bf16[1,768,768]{2,1,0:T(8,128)(2,1)} %bitcast.26, bf16[2,128,128]{2,1,0:T(8,128)(2,1)} %piv_ref.1, bf16[768,256]{1,0:T(8,128)(2,1)} %pad_maximum_fusion.v0, f32[1,768]{1,0:T(1,128)} %bitcast.25, ...), custom_call_target="tpu_custom_call" | custom-call | flops 6000000000 | bytes 5000000 | tf_op jit(solution)/shard_map/pallas_call | solution.py:368
  128.4 2.3 %copy.12 = bf16[1024,512]{1,0:T(8,128)(2,1)} copy(bf16[1024,512]{1,0:T(8,128)(2,1)} %shard_map.73) | data formatting | bytes 2097152
  (3 shorter events, 0.0 us)

commit v2 on v1

--- a/solution.py
+++ b/solution.py
@@ -18,16 +18,18 @@
 
 
 def fused_kernel(
-    col_count, l_ref, u_ref, d_ref, piv_ref, v0, flag_ref, keep_ref, pat_ref, hot_ref, out_ref,
-    lbuf, rbuf, pbuf, cin, xin, vy, vr, vl, vsr, vsl, s_acc, s_own, s_core, s_tot, s_x,
-    y_send, yv_send, zr_send, zl_send, vr_send, vl_send, l_recv, vy_recv, vr_recv, vl_recv,
+    col_count, l_ref, u_ref, d_ref, piv_ref, pat_ref, ord_ref, sep_ref, out_ref,
+    lbuf, rbuf, pbuf, cin, xin, v0, vbase, vy, vr, vl, vsr, vsl, s_acc, s_own, s_core, s_tot, s_x,
+    y_send, yb_send, yv_send, zr_send, zl_send, br_send, bl_send, vr_send, vl_send, l_recv, b_recv, vy_recv, vr_recv, vl_recv,
     c_send, c_recv, x_send, x_recv, s_send, s_recv,
 ):
     piece_rows, width = l_ref.shape
     cols = u_ref.shape[1]
     ext = rbuf.shape[1]
     nz = col_count // 2
+    blocks = cols // NB
     per_piece = piece_rows // NB
+    few = max(piece_rows // 8, 16)
     layer = lax.axis_index("layer")
     core, xx = layer % 2, layer // 2
     ci = lax.axis_index("col")
@@ -37,6 +39,17 @@
     y_peer = {"col": ci + 1 - 2 * y}
     right, left = {"col": ci + 2}, {"col": ci - 2}
     has_right, has_left = z < nz - 1, z > 0
+    first = ci * blocks
+
+    def one_if(condition):
+        return jnp.where(condition, 1.0, 0.0).astype(F32)
+
+    def hot_row(k, block):
+        return one_if(sep_ref[k] == block)
+
+    def hot_col(k, b):
+        return one_if(ord_ref[first + b] == sep_ref[k])
+
 
     def copy(src, dst, send, recv, peer):
         return pltpu.make_async_remote_copy(
@@ -58,15 +71,24 @@
     def _():
         pl.semaphore_signal(barrier, inc=1, device_id=left, device_id_type=MESH)
 
+    for k in range(2):
+        taken = u_ref[:, 0:NB].astype(F32) * hot_col(k, 0)
+        for b in range(1, blocks):
+            taken = taken + u_ref[:, b * NB : (b + 1) * NB].astype(F32) * hot_col(k, b)
+        v0[:, k * NB : (k + 1) * NB] = taken.astype(BF16)
+
     pl.semaphore_wait(barrier, 3 + jnp.where(has_right, 1, 0) + jnp.where(has_left, 1, 0))
 
-    parts = v0.shape[0] // (2 * NB)
+    parts = 4
+    part = v0.shape[0] // parts
+    y_first, z_first = (0, 1), (2, 3)
 
     def vpart(k):
-        return pl.ds(k * 2 * NB, 2 * NB)
+        return pl.ds(k * part, part)
 
     def v_y(k):
-        return copy(v0.at[vpart(k)], vy.at[vpart(k)], yv_send.at[k], vy_recv.at[k], y_peer)
+        src = v0 if k in y_first else vbase
+        return copy(src.at[vpart(k)], vy.at[vpart(k)], yv_send.at[k], vy_recv.at[k], y_peer)
 
     def v_right(k):
         return copy(vsr.at[vpart(k)], vr.at[vpart(k)], vr_send.at[k], vr_recv.at[k], right)
@@ -74,10 +96,60 @@
     def v_left(k):
         return copy(vsl.at[vpart(k)], vl.at[vpart(k)], vl_send.at[k], vl_recv.at[k], left)
 
-    for k in range(parts):
+    def add_right(k):
+        rows = vpart(k)
+
+        @pl.when(has_left)
+        def _():
+            v_right(k).wait_recv()
+            vsr[rows, :] = vsr[rows, :] + vr[rows, :]
+
+        @pl.when(has_right)
+        def _():
+            v_right(k).start()
+
+    def add_left(k):
+        rows = vpart(k)
+
+        @pl.when(has_right)
+        def _():
+            v_left(k).wait_recv()
+            vsl[rows, :] = vsl[rows, :] + vl[rows, :]
+
+        @pl.when(has_left)
+        def _():
+            v_left(k).start()
+
+    def near_way(k):
+        pl.when(z < nz // 2)(functools.partial(add_right, k))
+        pl.when(z >= nz // 2)(functools.partial(add_left, k))
+
+    def far_way(k):
+        pl.when(z < nz // 2)(functools.partial(add_left, k))
+        pl.when(z >= nz // 2)(functools.partial(add_right, k))
+
+    for k in y_first:
         v_y(k).start()
+    vsr[...] = v0[...]
+    vsl[...] = v0[...]
+
+    @pl.when(z == 0)
+    def _():
+        for k in z_first:
+            v_right(k).start()
+
+    @pl.when(z == nz - 1)
+    def _():
+        for k in z_first:
+            v_left(k).start()
 
     lbuf[piece(ci), :] = l_ref[...]
+
+    def head(p):
+        return pl.ds(pl.multiple_of(p * piece_rows, piece_rows), piece_rows - few)
+
+    def tail(p):
+        return pl.ds(pl.multiple_of(p * piece_rows + (piece_rows - few), few), few)
 
     def z_right(p):
         return copy(lbuf.at[piece(p)], lbuf.at[piece(p)], zr_send.at[p // 2], l_recv.at[p], right)
@@ -85,8 +157,19 @@
     def z_left(p):
         return copy(lbuf.at[piece(p)], lbuf.at[piece(p)], zl_send.at[p // 2], l_recv.at[p], left)
 
+    def tail_right(p):
+        return copy(lbuf.at[tail(p)], lbuf.at[tail(p)], br_send.at[p // 2], b_recv.at[p], right)
+
+    def tail_left(p):
+        return copy(lbuf.at[tail(p)], lbuf.at[tail(p)], bl_send.at[p // 2], b_recv.at[p], left)
+
     def over_y(p):
-        return copy(lbuf.at[piece(p)], lbuf.at[piece(p)], y_send.at[p // 2], l_recv.at[p], y_peer)
+        return copy(lbuf.at[head(p)], lbuf.at[head(p)], y_send.at[p // 2], l_recv.at[p], y_peer)
+
+    def tail_over_y(p):
+        return copy(lbuf.at[tail(p)], lbuf.at[tail(p)], yb_send.at[0], b_recv.at[p], y_peer)
+
+    tail_over_y(ci).start()
 
     @pl.when(has_right)
     def _():
@@ -102,67 +185,65 @@
     for s in range(supers):
         solved = dot(d_ref[s], u_ref[s * node : (s + 1) * node, :])
         rounded = solved.astype(BF16).astype(F32)
-        rbuf[s * node : (s + 1) * node, 0:cols] = (rounded * flag_ref[:, 0:cols]).astype(BF16)
-
-    for k in range(parts):
+        for b in range(blocks):
+            flag = -pat_ref[1, first + b].astype(F32)
+            rbuf[s * node : (s + 1) * node, b * NB : (b + 1) * NB] = (
+                rounded[:, b * NB : (b + 1) * NB] * flag
+            ).astype(BF16)
+
+    s_acc[...] = jnp.zeros_like(s_acc)
+
+    @pl.when((z > 0) & (z < nz - 1))
+    def _():
+        for k in z_first:
+            near_way(k)
+
+    for k in y_first:
         rows = vpart(k)
         v_y(k).wait_recv()
-        v0_sum = v0[rows, :] + vy[rows, :]
-        vsr[rows, :] = v0_sum
-        vsl[rows, :] = v0_sum
-
-        def go_right(k=k, rows=rows):
-            @pl.when(has_left)
-            def _():
-                v_right(k).wait_recv()
-                vsr[rows, :] = vsr[rows, :] + vr[rows, :]
-
-            @pl.when(has_right)
-            def _():
-                v_right(k).start()
-
-        def go_left(k=k, rows=rows):
-            @pl.when(has_right)
-            def _():
-                v_left(k).wait_recv()
-                vsl[rows, :] = vsl[rows, :] + vl[rows, :]
-
-            @pl.when(has_left)
-            def _():
-                v_left(k).start()
-
-        pl.when(z < nz // 2)(go_right)
-        pl.when(z >= nz // 2)(go_left)
-
-    for k in range(parts):
+        summed = v0[rows, :] + vy[rows, :]
+        vbase[rows, :] = summed
+        vsr[rows, :] = summed
+        vsl[rows, :] = summed
+        near_way(k)
+    for k in z_first:
         rows = vpart(k)
-
-        def go_right(k=k, rows=rows):
-            v_right(k).wait_recv()
-            vsr[rows, :] = vsr[rows, :] + vr[rows, :]
-
-            @pl.when(has_right)
-            def _():
-                v_right(k).start()
-
-        def go_left(k=k, rows=rows):
-            v_left(k).wait_recv()
-            vsl[rows, :] = vsl[rows, :] + vl[rows, :]
-
-            @pl.when(has_left)
-            def _():
-                v_left(k).start()
-
-        pl.when(z < nz // 2)(go_left)
-        pl.when(z >= nz // 2)(go_right)
-
-    vall = vsr[...] + vsl[...] - (v0[...] + vy[...])
+        far_way(k)
+        vbase[rows, :] = vsr[rows, :] + vsl[rows, :] - v0[rows, :]
+        v_y(k).start()
+    for k in y_first:
+        far_way(k)
+
+    other = ci + 1 - 2 * y
+    tail_over_y(other).wait_recv()
+
+    @pl.when(has_right)
+    def _():
+        tail_right(other).start()
+
+    @pl.when(has_left)
+    def _():
+        tail_left(other).start()
+
+    for k in z_first:
+        rows = vpart(k)
+        v_y(k).wait_recv()
+        v0[rows, :] = vbase[rows, :] + vy[rows, :]
+    for k in y_first:
+        rows = vpart(k)
+        v_y(k).wait_send()
+        v0[rows, :] = vsr[rows, :] + vsl[rows, :] - vbase[rows, :]
     for s in range(supers):
-        solved = dot(d_ref[s], vall[s * node : (s + 1) * node, :])
+        solved = dot(d_ref[s], v0[s * node : (s + 1) * node, :])
         rounded = solved.astype(BF16).astype(F32)
-        rbuf[s * node : (s + 1) * node, cols:ext] = (rounded * flag_ref[:, cols:ext]).astype(BF16)
-
-    s_acc[...] = jnp.zeros_like(s_acc)
+        for k in range(2):
+            held = jnp.int32(0)
+            for p in range(ord_ref.shape[0]):
+                held = held + jnp.where(ord_ref[p] == sep_ref[k], pat_ref[1, p], 0)
+            rbuf[s * node : (s + 1) * node, cols + k * NB : cols + (k + 1) * NB] = (
+                rounded[:, k * NB : (k + 1) * NB] * -held.astype(F32)
+            ).astype(BF16)
+
     per_span = col_count // 4
 
     def slot_of(p):
@@ -184,7 +265,7 @@
                 flagged = acc[j * NB : (j + 1) * NB] * pat_ref[0, block].astype(F32)
                 pbuf[pl.ds(pl.multiple_of(block * NB, NB), NB), n : n + 2 * NB] = flagged.astype(BF16)
                 for k in range(2):
-                    term = flagged * hot_ref[k, block]
+                    term = flagged * hot_row(k, block)
                     found[k] = term if j == 0 else found[k] + term
             for k in range(2):
                 s_acc[k * NB : (k + 1) * NB, n : n + 2 * NB] += found[k]
@@ -193,6 +274,9 @@
         @pl.when(span % 2 != core)
         def _():
             to_core(p).start()
+
+    def finish(p):
+        span = p // per_span
 
         @pl.when(span % 2 == core)
         def _():
@@ -209,43 +293,51 @@
             def _():
                 to_x(p).start()
 
-    def place(i):
-        dist = (i + 1) // 2
-        return z + dist * (1 - 2 * (i % 2))
-
-    events = 2 * nz - 1
-
-    @pl.loop(0, events + 2)
-    def _(i):
-        zc = place(i)
-
-        @pl.when((i < events) & (zc >= 0) & (zc < nz))
-        def _():
-            p = zc * 2 + y
-
-            @pl.when(i > 0)
+    @pl.loop(0, nz)
+    def _(step):
+        for way in (1, -1):
+            zc = z + way * (step + 1)
+
+            @pl.when((zc >= 0) & (zc < nz))
+            def _(zc=zc, way=way):
+                p, o = zc * 2 + y, zc * 2 + 1 - y
+                z_right(p).wait_recv()
+                on = has_left if way > 0 else has_right
+
+                @pl.when(on)
+                def _():
+                    (z_left if way > 0 else z_right)(p).start()
+
+                over_y(p).start()
+                tail_right(o).wait_recv()
+
+                @pl.when(on)
+                def _():
+                    (tail_left if way > 0 else tail_right)(o).start()
+
+        def candidate(t):
+            zc = z + step * (1 - 2 * (t % 2))
+            line = jnp.where(t < 2, y, 1 - y)
+            valid = (zc >= 0) & (zc < nz) & ((step > 0) | (t % 2 == 0))
+            return zc * 2 + line, valid
+
+        @pl.loop(0, 5)
+        def _(t):
+            p, valid = candidate(t)
+
+            @pl.when((t < 4) & valid)
             def _():
-                over_y(p).wait_recv()
-
-                @pl.when(has_right & (zc < z))
+                @pl.when(t >= 2)
                 def _():
-                    z_right(p).start()
-
-                @pl.when(has_left & (zc > z))
-                def _():
-                    z_left(p).start()
-
-                over_y(p).start()
-
-            process(p)
-
-        zo = place(jnp.maximum(i - 2, 0))
-
-        @pl.when((i >= 2) & (zo >= 0) & (zo < nz))
-        def _():
-            p = zo * 2 + 1 - y
-            over_y(p).wait_recv()
-            process(p)
+                    over_y(p).wait_recv()
+
+                process(p)
+
+            before, valid_before = candidate(jnp.maximum(t - 1, 0))
+
+            @pl.when((t > 0) & valid_before)
+            def _():
+                finish(before)
 
     def s_copy(src, dst, k, peer):
         return copy(src, dst, s_send.at[k], s_recv.at[k], peer)
@@ -266,7 +358,10 @@
     pos_col = [cols, cols + NB]
     upper = jnp.concatenate([s_tot[0:NB, 0:cols], s_x[0:NB, 0:cols]], axis=0)
     upper_p = jnp.concatenate([s_tot[0:NB, pos_col[1] : ext], s_x[0:NB, pos_col[1] : ext]], axis=0)
-    keep_c = [keep_ref[k : k + 1, :] for k in range(2)]
+    keep_c = [
+        jnp.concatenate([jnp.full((1, NB), 1.0, F32) * (1.0 - hot_col(k, b)) for b in range(blocks)], axis=1)
+        for k in range(2)
+    ]
 
     def factors(a, b):
         return jnp.concatenate([dot(a, piv_ref[0]).astype(BF16), dot(b, piv_ref[0]).astype(BF16)], axis=1)
@@ -284,7 +379,7 @@
 
         def keep_rows(value, k):
             kept = [
-                value[j * NB : (j + 1) * NB] * (1.0 - hot_ref[k, p * per_piece + j]) for j in range(per_piece)
+                value[j * NB : (j + 1) * NB] * (1.0 - hot_row(k, p * per_piece + j)) for j in range(per_piece)
             ]
             return jnp.concatenate(kept, axis=0)
 
@@ -299,7 +394,8 @@
     over_x.wait_send()
     share.wait_send()
     for k in range(parts):
-        v_y(k).wait_send()
+        if k in z_first:
+            v_y(k).wait_send()
 
         @pl.when(has_right)
         def _():
@@ -308,19 +404,23 @@
         @pl.when(has_left)
         def _():
             v_left(k).wait_send()
+
+    tail_over_y(ci).wait_send()
 
     @pl.loop(0, nz)
     def _(zc):
-        p = zc * 2 + y
+        p, o = zc * 2 + y, zc * 2 + 1 - y
         over_y(p).wait_send()
 
         @pl.when(has_right & (zc <= z))
         def _():
             z_right(p).wait_send()
+            tail_right(o).wait_send()
 
         @pl.when(has_left & (zc >= z))
         def _():
             z_left(p).wait_send()
+            tail_left(o).wait_send()
 
     @pl.loop(0, col_count)
     def _(p):
@@ -343,23 +443,7 @@
     nz, slots = col_count // 2, col_count // 2
     total_rows = piece_rows * col_count
     per_span = col_count // 4
-    parts = width // (2 * NB)
-    positions = jnp.arange(col_order.shape[0], dtype=jnp.int32)
-    pos = jnp.sum(jnp.where(col_order[None, :] == sep_blocks[:, None], positions[None, :], 0), axis=1)
-    blocks = cols // NB
-    first = lax.axis_index("col") * blocks
-    masked = []
-    for k in range(2):
-        local = pos[k] - first
-        inside = (local >= 0) & (local < blocks)
-        taken = lax.dynamic_slice_in_dim(upper_panel[0], jnp.clip(local, 0, blocks - 1) * NB, NB, 1)
-        masked.append(jnp.where(inside, taken, jnp.zeros_like(taken)))
-    masked = jnp.concatenate(masked, axis=1)
-    own_flags = lax.dynamic_slice_in_dim(pattern[0, 1], first, blocks)
-    flags = -jnp.repeat(jnp.concatenate([own_flags, pattern[0, 1][pos]]), NB)[None, :].astype(F32)
-    col_block = first + jnp.arange(cols, dtype=jnp.int32) // NB
-    keep = (col_block[None, :] != pos[:, None]).astype(F32)
-    hot = (positions[None, :] == sep_blocks[:, None]).astype(F32)
+    parts = 4
     vmem = pl.BlockSpec(memory_space=pltpu.VMEM)
     smem = pl.BlockSpec(memory_space=pltpu.SMEM)
     dma = pltpu.SemaphoreType.DMA
@@ -368,7 +452,7 @@
     return pl.pallas_call(
         functools.partial(fused_kernel, col_count),
         out_shape=jax.ShapeDtypeStruct((per_span * piece_rows, cols), BF16),
-        in_specs=[vmem] * 7 + [smem] * 2,
+        in_specs=[vmem] * 4 + [smem] * 3,
         out_specs=vmem,
         scratch_shapes=[
             pltpu.VMEM((total_rows, width), BF16),
@@ -376,10 +460,10 @@
             pltpu.VMEM((total_rows, ext), BF16),
             pltpu.VMEM((slots, piece_rows, ext), BF16),
             pltpu.VMEM((per_span, piece_rows, ext), BF16),
-            v_shape, v_shape, v_shape, v_shape, v_shape,
+            v_shape, v_shape, v_shape, v_shape, v_shape, v_shape, v_shape,
             pltpu.VMEM((2 * NB, ext), F32), s_shape, s_shape, s_shape, s_shape,
-            dma((nz,)), dma((parts,)), dma((nz,)), dma((nz,)), dma((parts,)), dma((parts,)),
-            dma((col_count,)), dma((parts,)), dma((parts,)), dma((parts,)),
+            dma((nz,)), dma((1,)), dma((parts,)), dma((nz,)), dma((nz,)), dma((nz,)), dma((nz,)), dma((parts,)), dma((parts,)),
+            dma((col_count,)), dma((col_count,)), dma((parts,)), dma((parts,)), dma((parts,)),
             dma((slots,)), dma((slots,)), dma((per_span,)), dma((per_span,)), dma((3,)), dma((3,)),
         ],
         compiler_params=pltpu.CompilerParams(
@@ -387,8 +471,8 @@
         ),
         cost_estimate=pl.CostEstimate(flops=6 * 10**9, bytes_accessed=5 * 10**6, transcendentals=0),
     )(
-        lower_panel[0], upper_panel[0], diag_inverse[0], pivot_inverse, masked, flags, keep,
-        pattern[0], hot,
+        lower_panel[0], upper_panel[0], diag_inverse[0], pivot_inverse, pattern[0], col_order,
+        sep_blocks,
     )
 
 

time: 131 us -> 133 us (1.015)
  Pallas kernels: 120 us -> 130 us
  other arithmetic: 4.8 us -> 0 us
  local copies, waits for them, and re-layouts: 4.89 us -> 2.26 us
    pallas_call x1, Pallas kernels: 120 us -> 130 us  [fused(): pl.pallas_call(functools.partial(fused_kernel, col_count), out_shape=jax....]
    convert_element_type x2 -> x0, other arithmetic: 1.96 us -> none  [the longest x1 1.3 us: fused(): hot = (positions[None, :] == sep_blocks[:, None]).astype(F32)]
    unnamed x3 -> x1, local copies, waits for them, and re-layouts: 2.92 us -> 2.26 us
where the time goes in v2:
time: 133 us; the launch traced here: 132 us
  Pallas kernels  130 us (98%)
  local copies, waits for them, and re-layouts  2.26 us (2%)
    pallas_call x1, Pallas kernels, fused(): pl.pallas_call(functools.partial(fused_kernel, col_count), out_shape=jax....  130 us

profile of v2, /device:TPU:25, one launch (start us, length us, event | category | flops | bytes accessed | tf_op | source)
XLA Modules:
  0.0 132.0 jit_solution(5102442587514502073)
XLA Ops:
  0.0 129.7 %shard_map.73 = bf16[1024,512]{1,0:T(8,128)(2,1)} custom-call(bf16[512,768]{1,0:T(8,128)(2,1)} %bitcast.5, bf16[768,512]{1,0:T(8,128)(2,1)} %bitcast.6, bf16[1,768,768]{2,1,0:T(8,128)(2,1)} %bitcast.4, bf16[2,128,128]{2,1,0:T(8,128)(2,1)} %piv_ref.1, s32[2,32]{1,0:T(2,128)} %bitcast.7, s32[32]{0:T(128)} %ord_ref.1, s32[2]{0:T(128)} %sep_ref.1), custom_call_target="tpu_custom_call" | custom-call | flops 6000000000 | bytes 5000000 | tf_op jit(solution)/shard_map/pallas_call | solution.py:452
  129.7 2.3 %copy.9 = bf16[1024,512]{1,0:T(8,128)(2,1)} copy(bf16[1024,512]{1,0:T(8,128)(2,1)} %shard_map.73) | data formatting | bytes 2097152

commit v3 on v2

--- a/solution.py
+++ b/solution.py
@@ -24,12 +24,13 @@
     c_send, c_recv, x_send, x_recv, s_send, s_recv,
 ):
     piece_rows, width = l_ref.shape
+    half = piece_rows // 2
     cols = u_ref.shape[1]
     ext = rbuf.shape[1]
     nz = col_count // 2
     blocks = cols // NB
-    per_piece = piece_rows // NB
-    few = max(piece_rows // 8, 16)
+    per_half = half // NB
+    few = max(piece_rows // 16, 16)
     layer = lax.axis_index("layer")
     core, xx = layer % 2, layer // 2
     ci = lax.axis_index("col")
@@ -59,6 +60,9 @@
     def piece(p):
         return pl.ds(pl.multiple_of(p * piece_rows, piece_rows), piece_rows)
 
+    def chunk(q):
+        return pl.ds(pl.multiple_of(q * half, half), half)
+
     barrier = pltpu.get_barrier_semaphore()
     for peer in (core_peer, x_peer, y_peer):
         pl.semaphore_signal(barrier, inc=1, device_id=peer, device_id_type=MESH)
@@ -145,17 +149,19 @@
 
     lbuf[piece(ci), :] = l_ref[...]
 
-    def head(p):
-        return pl.ds(pl.multiple_of(p * piece_rows, piece_rows), piece_rows - few)
+    def head(p, h):
+        return pl.ds(pl.multiple_of(p * piece_rows + h * half, half), half - few * h)
 
     def tail(p):
         return pl.ds(pl.multiple_of(p * piece_rows + (piece_rows - few), few), few)
 
-    def z_right(p):
-        return copy(lbuf.at[piece(p)], lbuf.at[piece(p)], zr_send.at[p // 2], l_recv.at[p], right)
-
-    def z_left(p):
-        return copy(lbuf.at[piece(p)], lbuf.at[piece(p)], zl_send.at[p // 2], l_recv.at[p], left)
+    def z_right(p, h):
+        rows = chunk(2 * p + h)
+        return copy(lbuf.at[rows], lbuf.at[rows], zr_send.at[p // 2 * 2 + h], l_recv.at[2 * p + h], right)
+
+    def z_left(p, h):
+        rows = chunk(2 * p + h)
+        return copy(lbuf.at[rows], lbuf.at[rows], zl_send.at[p // 2 * 2 + h], l_recv.at[2 * p + h], left)
 
     def tail_right(p):
         return copy(lbuf.at[tail(p)], lbuf.at[tail(p)], br_send.at[p // 2], b_recv.at[p], right)
@@ -163,33 +169,16 @@
     def tail_left(p):
         return copy(lbuf.at[tail(p)], lbuf.at[tail(p)], bl_send.at[p // 2], b_recv.at[p], left)
 
-    def over_y(p):
-        return copy(lbuf.at[head(p)], lbuf.at[head(p)], y_send.at[p // 2], l_recv.at[p], y_peer)
+    def over_y(p, h):
+        rows = head(p, h)
+        return copy(lbuf.at[rows], lbuf.at[rows], y_send.at[p // 2 * 2 + h], l_recv.at[2 * p + h], y_peer)
 
     def tail_over_y(p):
         return copy(lbuf.at[tail(p)], lbuf.at[tail(p)], yb_send.at[0], b_recv.at[p], y_peer)
 
     tail_over_y(ci).start()
-
-    @pl.when(has_right)
-    def _():
-        z_right(ci).start()
-
-    @pl.when(has_left)
-    def _():
-        z_left(ci).start()
-
-    over_y(ci).start()
-
-    supers, node = d_ref.shape[0], d_ref.shape[1]
-    for s in range(supers):
-        solved = dot(d_ref[s], u_ref[s * node : (s + 1) * node, :])
-        rounded = solved.astype(BF16).astype(F32)
-        for b in range(blocks):
-            flag = -pat_ref[1, first + b].astype(F32)
-            rbuf[s * node : (s + 1) * node, b * NB : (b + 1) * NB] = (
-                rounded[:, b * NB : (b + 1) * NB] * flag
-            ).astype(BF16)
+    for h in range(2):
+        over_y(ci, h).start()
 
     s_acc[...] = jnp.zeros_like(s_acc)
 
@@ -214,6 +203,16 @@
     for k in y_first:
         far_way(k)
 
+    for h in range(2):
+
+        @pl.when(has_right)
+        def _():
+            z_right(ci, h).start()
+
+        @pl.when(has_left)
+        def _():
+            z_left(ci, h).start()
+
     other = ci + 1 - 2 * y
     tail_over_y(other).wait_recv()
 
@@ -224,6 +223,16 @@
     @pl.when(has_left)
     def _():
         tail_left(other).start()
+
+    supers, node = d_ref.shape[0], d_ref.shape[1]
+    for s in range(supers):
+        solved = dot(d_ref[s], u_ref[s * node : (s + 1) * node, :])
+        rounded = solved.astype(BF16).astype(F32)
+        for b in range(blocks):
+            flag = -pat_ref[1, first + b].astype(F32)
+            rbuf[s * node : (s + 1) * node, b * NB : (b + 1) * NB] = (
+                rounded[:, b * NB : (b + 1) * NB] * flag
+            ).astype(BF16)
 
     for k in z_first:
         rows = vpart(k)
@@ -246,22 +255,26 @@
 
     per_span = col_count // 4
 
-    def slot_of(p):
-        return (p // per_span // 2) * per_span + p % per_span
-
-    def to_core(p):
-        return copy(pbuf.at[piece(p)], cin.at[slot_of(p)], c_send.at[slot_of(p)], c_recv.at[slot_of(p)], core_peer)
-
-    def to_x(p):
-        return copy(pbuf.at[piece(p)], xin.at[p % per_span], x_send.at[p % per_span], x_recv.at[p % per_span], x_peer)
-
-    def process(p):
-        rows = lbuf[piece(p), :]
+    span_halves = 2 * per_span
+
+    def slot_of(q):
+        return q // span_halves // 2 * span_halves + q % span_halves
+
+    def to_core(q):
+        slot = slot_of(q)
+        return copy(pbuf.at[chunk(q)], cin.at[slot], c_send.at[slot], c_recv.at[slot], core_peer)
+
+    def to_x(q):
+        slot = q % span_halves
+        return copy(pbuf.at[chunk(q)], xin.at[slot], x_send.at[slot], x_recv.at[slot], x_peer)
+
+    def process(q):
+        rows = lbuf[chunk(q), :]
         for n in range(0, ext, 2 * NB):
             acc = dot(rows, rbuf[:, n : n + 2 * NB])
             found = [None, None]
-            for j in range(per_piece):
-                block = p * per_piece + j
+            for j in range(per_half):
+                block = q * per_half + j
                 flagged = acc[j * NB : (j + 1) * NB] * pat_ref[0, block].astype(F32)
                 pbuf[pl.ds(pl.multiple_of(block * NB, NB), NB), n : n + 2 * NB] = flagged.astype(BF16)
                 for k in range(2):
@@ -269,75 +282,81 @@
                     found[k] = term if j == 0 else found[k] + term
             for k in range(2):
                 s_acc[k * NB : (k + 1) * NB, n : n + 2 * NB] += found[k]
-        span = p // per_span
+        span = q // span_halves
 
         @pl.when(span % 2 != core)
         def _():
-            to_core(p).start()
-
-    def finish(p):
-        span = p // per_span
+            to_core(q).start()
+
+    def finish(q):
+        span = q // span_halves
 
         @pl.when(span % 2 == core)
         def _():
-            to_core(p).wait_recv()
-            slot = slot_of(p)
-
-            @pl.loop(0, per_piece)
+            to_core(q).wait_recv()
+            slot = slot_of(q)
+
+            @pl.loop(0, per_half)
             def _(j):
-                at = pl.ds(pl.multiple_of(p * piece_rows + j * NB, NB), NB)
+                at = pl.ds(pl.multiple_of(q * half + j * NB, NB), NB)
                 here = pl.ds(pl.multiple_of(j * NB, NB), NB)
                 pbuf[at, :] = (pbuf[at, :].astype(F32) + cin[slot, here, :].astype(F32)).astype(BF16)
 
             @pl.when(span // 2 != xx)
             def _():
-                to_x(p).start()
+                to_x(q).start()
 
     @pl.loop(0, nz)
     def _(step):
-        for way in (1, -1):
-            zc = z + way * (step + 1)
-
-            @pl.when((zc >= 0) & (zc < nz))
-            def _(zc=zc, way=way):
-                p, o = zc * 2 + y, zc * 2 + 1 - y
-                z_right(p).wait_recv()
-                on = has_left if way > 0 else has_right
-
-                @pl.when(on)
-                def _():
-                    (z_left if way > 0 else z_right)(p).start()
-
-                over_y(p).start()
-                tail_right(o).wait_recv()
-
-                @pl.when(on)
-                def _():
-                    (tail_left if way > 0 else tail_right)(o).start()
+        for h in range(2):
+            for way in (1, -1):
+                zc = z + way * (step + 1)
+
+                @pl.when((zc >= 0) & (zc < nz))
+                def _(zc=zc, way=way, h=h):
+                    p, o = zc * 2 + y, zc * 2 + 1 - y
+                    z_right(p, h).wait_recv()
+                    on = has_left if way > 0 else has_right
+
+                    @pl.when(on)
+                    def _():
+                        (z_left if way > 0 else z_right)(p, h).start()
+
+                    over_y(p, h).start()
+                    if h == 1:
+                        tail_right(o).wait_recv()
+
+                        @pl.when(on)
+                        def _():
+                            (tail_left if way > 0 else tail_right)(o).start()
 
         def candidate(t):
             zc = z + step * (1 - 2 * (t % 2))
-            line = jnp.where(t < 2, y, 1 - y)
+            line = jnp.where(t < 4, y, 1 - y)
             valid = (zc >= 0) & (zc < nz) & ((step > 0) | (t % 2 == 0))
-            return zc * 2 + line, valid
-
-        @pl.loop(0, 5)
+            return zc * 2 + line, (t // 2) % 2, valid
+
+        @pl.loop(0, 9)
         def _(t):
-            p, valid = candidate(t)
-
-            @pl.when((t < 4) & valid)
+            p, h, valid = candidate(t)
+
+            @pl.when((t < 8) & valid)
             def _():
-                @pl.when(t >= 2)
+                @pl.when((t >= 4) & (h == 0))
                 def _():
-                    over_y(p).wait_recv()
-
-                process(p)
-
-            before, valid_before = candidate(jnp.maximum(t - 1, 0))
+                    over_y(p, 0).wait_recv()
+
+                @pl.when((t >= 4) & (h == 1))
+                def _():
+                    over_y(p, 1).wait_recv()
+
+                process(2 * p + h)
+
+            p_before, h_before, valid_before = candidate(jnp.maximum(t - 1, 0))
 
             @pl.when((t > 0) & valid_before)
             def _():
-                finish(before)
+                finish(2 * p_before + h_before)
 
     def s_copy(src, dst, k, peer):
         return copy(src, dst, s_send.at[k], s_recv.at[k], peer)
@@ -370,26 +389,26 @@
     last = s_tot[NB : 2 * NB, 0:cols].astype(F32) + s_x[NB : 2 * NB, 0:cols].astype(F32)
     upper2 = ((last - dot(fs, upper)) * keep_c[0]).astype(BF16)
 
-    for q in range(per_span):
-        p = layer * per_span + q
-
-        to_x(p).wait_recv()
-        at = piece(p)
-        f0 = factors(pbuf[at, cols : cols + NB], xin[q, :, cols : cols + NB])
+    for slot in range(span_halves):
+        q = layer * span_halves + slot
+
+        to_x(q).wait_recv()
+        at = chunk(q)
+        f0 = factors(pbuf[at, cols : cols + NB], xin[slot, :, cols : cols + NB])
 
         def keep_rows(value, k):
             kept = [
-                value[j * NB : (j + 1) * NB] * (1.0 - hot_row(k, p * per_piece + j)) for j in range(per_piece)
+                value[j * NB : (j + 1) * NB] * (1.0 - hot_row(k, q * per_half + j)) for j in range(per_half)
             ]
             return jnp.concatenate(kept, axis=0)
 
-        panel = pbuf[at, pos_col[1] : ext].astype(F32) + xin[q, :, pos_col[1] : ext].astype(F32)
+        panel = pbuf[at, pos_col[1] : ext].astype(F32) + xin[slot, :, pos_col[1] : ext].astype(F32)
         panel = keep_rows(panel - dot(f0, upper_p), 0).astype(BF16)
         f2 = dot(panel, piv_ref[1]).astype(BF16)
-        total = pbuf[at, 0:cols].astype(F32) + xin[q, :, 0:cols].astype(F32)
+        total = pbuf[at, 0:cols].astype(F32) + xin[slot, :, 0:cols].astype(F32)
         total = keep_rows(total - dot(f0, upper), 0) * keep_c[0]
         final = keep_rows(total - dot(f2, upper2), 1) * keep_c[1]
-        out_ref[q * piece_rows : (q + 1) * piece_rows, :] = final.astype(BF16)
+        out_ref[slot * half : (slot + 1) * half, :] = final.astype(BF16)
 
     over_x.wait_send()
     share.wait_send()
@@ -410,29 +429,36 @@
     @pl.loop(0, nz)
     def _(zc):
         p, o = zc * 2 + y, zc * 2 + 1 - y
-        over_y(p).wait_send()
+        for h in range(2):
+            over_y(p, h).wait_send()
+
+            @pl.when(has_right & (zc <= z))
+            def _():
+                z_right(p, h).wait_send()
+
+            @pl.when(has_left & (zc >= z))
+            def _():
+                z_left(p, h).wait_send()
 
         @pl.when(has_right & (zc <= z))
         def _():
-            z_right(p).wait_send()
             tail_right(o).wait_send()
 
         @pl.when(has_left & (zc >= z))
         def _():
-            z_left(p).wait_send()
             tail_left(o).wait_send()
 
-    @pl.loop(0, col_count)
-    def _(p):
-        span = p // per_span
+    @pl.loop(0, 2 * col_count)
+    def _(q):
+        span = q // span_halves
 
         @pl.when(span % 2 != core)
         def _():
-            to_core(p).wait_send()
+            to_core(q).wait_send()
 
         @pl.when((span % 2 == core) & (span // 2 != xx))
         def _():
-            to_x(p).wait_send()
+            to_x(q).wait_send()
 
 
 def fused(lower_panel, upper_panel, diag_inverse, pivot_inverse, pattern, col_order, sep_blocks):
@@ -440,7 +466,7 @@
     piece_rows, width = lower_panel.shape[1:]
     cols = upper_panel.shape[2]
     ext = cols + 2 * NB
-    nz, slots = col_count // 2, col_count // 2
+    nz, slots, half = col_count // 2, col_count, piece_rows // 2
     total_rows = piece_rows * col_count
     per_span = col_count // 4
     parts = 4
@@ -458,13 +484,13 @@
             pltpu.VMEM((total_rows, width), BF16),
             pltpu.VMEM((width, ext), BF16),
             pltpu.VMEM((total_rows, ext), BF16),
-            pltpu.VMEM((slots, piece_rows, ext), BF16),
-            pltpu.VMEM((per_span, piece_rows, ext), BF16),
+            pltpu.VMEM((slots, half, ext), BF16),
+            pltpu.VMEM((2 * per_span, half, ext), BF16),
             v_shape, v_shape, v_shape, v_shape, v_shape, v_shape, v_shape,
             pltpu.VMEM((2 * NB, ext), F32), s_shape, s_shape, s_shape, s_shape,
-            dma((nz,)), dma((1,)), dma((parts,)), dma((nz,)), dma((nz,)), dma((nz,)), dma((nz,)), dma((parts,)), dma((parts,)),
-            dma((col_count,)), dma((col_count,)), dma((parts,)), dma((parts,)), dma((parts,)),
-            dma((slots,)), dma((slots,)), dma((per_span,)), dma((per_span,)), dma((3,)), dma((3,)),
+            dma((2 * nz,)), dma((1,)), dma((parts,)), dma((2 * nz,)), dma((2 * nz,)), dma((nz,)), dma((nz,)), dma((parts,)), dma((parts,)),
+            dma((2 * col_count,)), dma((col_count,)), dma((parts,)), dma((parts,)), dma((parts,)),
+            dma((slots,)), dma((slots,)), dma((2 * per_span,)), dma((2 * per_span,)), dma((3,)), dma((3,)),
         ],
         compiler_params=pltpu.CompilerParams(
             collective_id=0, has_side_effects=True, vmem_limit_bytes=56 * 2**20
@@ -576,7 +602,7 @@
     return (
         layers == 4
         and columns % layers == 0
-        and rows % NB == 0
+        and rows % (2 * NB) == 0
         and cols % (2 * NB) == 0
         and width % (2 * NB) == 0
         and diag_inverse.shape[2] % NB == 0

time: 133 us -> 128 us (0.962)
  Pallas kernels: 130 us -> 126 us
    pallas_call x1, Pallas kernels: 130 us -> 126 us  [fused(): pl.pallas_call(functools.partial(fused_kernel, col_count), out_shape=jax....]
where the time goes in v3:
time: 128 us
  Pallas kernels  126 us (98%)
  local copies, waits for them, and re-layouts  2.26 us (2%)
    pallas_call x1, Pallas kernels, fused(): pl.pallas_call(functools.partial(fused_kernel, col_count), out_shape=jax....  126 us

profile of v3, /device:TPU:25, one launch (start us, length us, event | category | flops | bytes accessed | tf_op | source)
XLA Modules:
  0.0 128.0 jit_solution(13217682848855614971)
XLA Ops:
  0.0 125.8 %shard_map.73 = bf16[1024,512]{1,0:T(8,128)(2,1)} custom-call(bf16[512,768]{1,0:T(8,128)(2,1)} %bitcast.5, bf16[768,512]{1,0:T(8,128)(2,1)} %bitcast.6, bf16[1,768,768]{2,1,0:T(8,128)(2,1)} %bitcast.4, bf16[2,128,128]{2,1,0:T(8,128)(2,1)} %piv_ref.1, s32[2,32]{1,0:T(2,128)} %bitcast.7, s32[32]{0:T(128)} %ord_ref.1, s32[2]{0:T(128)} %sep_ref.1), custom_call_target="tpu_custom_call" | custom-call | flops 6000000000 | bytes 5000000 | tf_op jit(solution)/shard_map/pallas_call | solution.py:478
  125.8 2.3 %copy.9 = bf16[1024,512]{1,0:T(8,128)(2,1)} copy(bf16[1024,512]{1,0:T(8,128)(2,1)} %shard_map.73) | data formatting | bytes 2097152

commit v4 on v3

--- a/solution.py
+++ b/solution.py
@@ -306,8 +306,40 @@
             def _():
                 to_x(q).start()
 
+    def handle(step, line, arriving):
+        def candidate(t):
+            zc = z + step * (1 - 2 * (t % 2))
+            valid = (zc >= 0) & (zc < nz) & ((step > 0) | (t % 2 == 0))
+            return zc * 2 + line, t // 2, valid
+
+        @pl.loop(0, 6)
+        def _(t):
+            p, h, valid = candidate(t)
+
+            @pl.when((t < 4) & valid)
+            def _():
+                if arriving:
+
+                    @pl.when(h == 0)
+                    def _():
+                        over_y(p, 0).wait_recv()
+
+                    @pl.when(h == 1)
+                    def _():
+                        over_y(p, 1).wait_recv()
+
+                process(2 * p + h)
+
+            p_before, h_before, valid_before = candidate(jnp.maximum(t - 2, 0))
+
+            @pl.when((t >= 2) & valid_before)
+            def _():
+                finish(2 * p_before + h_before)
+
     @pl.loop(0, nz)
     def _(step):
+        handle(step, y, False)
+
         for h in range(2):
             for way in (1, -1):
                 zc = z + way * (step + 1)
@@ -330,33 +362,7 @@
                         def _():
                             (tail_left if way > 0 else tail_right)(o).start()
 
-        def candidate(t):
-            zc = z + step * (1 - 2 * (t % 2))
-            line = jnp.where(t < 4, y, 1 - y)
-            valid = (zc >= 0) & (zc < nz) & ((step > 0) | (t % 2 == 0))
-            return zc * 2 + line, (t // 2) % 2, valid
-
-        @pl.loop(0, 9)
-        def _(t):
-            p, h, valid = candidate(t)
-
-            @pl.when((t < 8) & valid)
-            def _():
-                @pl.when((t >= 4) & (h == 0))
-                def _():
-                    over_y(p, 0).wait_recv()
-
-                @pl.when((t >= 4) & (h == 1))
-                def _():
-                    over_y(p, 1).wait_recv()
-
-                process(2 * p + h)
-
-            p_before, h_before, valid_before = candidate(jnp.maximum(t - 1, 0))
-
-            @pl.when((t > 0) & valid_before)
-            def _():
-                finish(2 * p_before + h_before)
+        handle(step, 1 - y, True)
 
     def s_copy(src, dst, k, peer):
         return copy(src, dst, s_send.at[k], s_recv.at[k], peer)

time: 128 us -> 120 us (0.938)
  Pallas kernels: 126 us -> 117 us
    pallas_call x1, Pallas kernels: 126 us -> 117 us  [fused(): pl.pallas_call(functools.partial(fused_kernel, col_count), out_shape=jax....]
where the time goes in v4:
time: 120 us
  Pallas kernels  117 us (98%)
  local copies, waits for them, and re-layouts  2.26 us (2%)
    pallas_call x1, Pallas kernels, fused(): pl.pallas_call(functools.partial(fused_kernel, col_count), out_shape=jax....  117 us

profile of v4, /device:TPU:25, one launch (start us, length us, event | category | flops | bytes accessed | tf_op | source)
XLA Modules:
  0.0 119.6 jit_solution(18387708282782349991)
XLA Ops:
  0.0 117.3 %shard_map.73 = bf16[1024,512]{1,0:T(8,128)(2,1)} custom-call(bf16[512,768]{1,0:T(8,128)(2,1)} %bitcast.5, bf16[768,512]{1,0:T(8,128)(2,1)} %bitcast.6, bf16[1,768,768]{2,1,0:T(8,128)(2,1)} %bitcast.4, bf16[2,128,128]{2,1,0:T(8,128)(2,1)} %piv_ref.1, s32[2,32]{1,0:T(2,128)} %bitcast.7, s32[32]{0:T(128)} %ord_ref.1, s32[2]{0:T(128)} %sep_ref.1), custom_call_target="tpu_custom_call" | custom-call | flops 6000000000 | bytes 5000000 | tf_op jit(solution)/shard_map/pallas_call | solution.py:484
  117.3 2.3 %copy.9 = bf16[1024,512]{1,0:T(8,128)(2,1)} copy(bf16[1024,512]{1,0:T(8,128)(2,1)} %shard_map.73) | data formatting | bytes 2097152

commit v5 on v4

--- a/solution.py
+++ b/solution.py
@@ -180,6 +180,14 @@
     for h in range(2):
         over_y(ci, h).start()
 
+        @pl.when(has_right)
+        def _():
+            z_right(ci, h).start()
+
+        @pl.when(has_left)
+        def _():
+            z_left(ci, h).start()
+
     s_acc[...] = jnp.zeros_like(s_acc)
 
     @pl.when((z > 0) & (z < nz - 1))
@@ -203,16 +211,6 @@
     for k in y_first:
         far_way(k)
 
-    for h in range(2):
-
-        @pl.when(has_right)
-        def _():
-            z_right(ci, h).start()
-
-        @pl.when(has_left)
-        def _():
-            z_left(ci, h).start()
-
     other = ci + 1 - 2 * y
     tail_over_y(other).wait_recv()
 
@@ -223,6 +221,31 @@
     @pl.when(has_left)
     def _():
         tail_left(other).start()
+
+    def pass_on(step):
+        for h in range(2):
+            for way in (1, -1):
+                zc = z + way * (step + 1)
+
+                @pl.when((zc >= 0) & (zc < nz))
+                def _(zc=zc, way=way, h=h):
+                    p, o = zc * 2 + y, zc * 2 + 1 - y
+                    z_right(p, h).wait_recv()
+                    on = has_left if way > 0 else has_right
+
+                    @pl.when(on)
+                    def _():
+                        (z_left if way > 0 else z_right)(p, h).start()
+
+                    over_y(p, h).start()
+                    if h == 1:
+                        tail_right(o).wait_recv()
+
+                        @pl.when(on)
+                        def _():
+                            (tail_left if way > 0 else tail_right)(o).start()
+
+    pass_on(0)
 
     supers, node = d_ref.shape[0], d_ref.shape[1]
     for s in range(supers):
@@ -340,27 +363,9 @@
     def _(step):
         handle(step, y, False)
 
-        for h in range(2):
-            for way in (1, -1):
-                zc = z + way * (step + 1)
-
-                @pl.when((zc >= 0) & (zc < nz))
-                def _(zc=zc, way=way, h=h):
-                    p, o = zc * 2 + y, zc * 2 + 1 - y
-                    z_right(p, h).wait_recv()
-                    on = has_left if way > 0 else has_right
-
-                    @pl.when(on)
-                    def _():
-                        (z_left if way > 0 else z_right)(p, h).start()
-
-                    over_y(p, h).start()
-                    if h == 1:
-                        tail_right(o).wait_recv()
-
-                        @pl.when(on)
-                        def _():
-                            (tail_left if way > 0 else tail_right)(o).start()
+        @pl.when(step > 0)
+        def _():
+            pass_on(step)
 
         handle(step, 1 - y, True)
 

time: 120 us -> 120 us (level)
  no operation moved by 1% of the time
where the time goes in v5:
time: 120 us
  Pallas kernels  117 us (98%)
  local copies, waits for them, and re-layouts  2.26 us (2%)
    pallas_call x1, Pallas kernels, fused(): pl.pallas_call(functools.partial(fused_kernel, col_count), out_shape=jax....  117 us

profile of v5, /device:TPU:25, one launch (start us, length us, event | category | flops | bytes accessed | tf_op | source)
XLA Modules:
  0.0 119.5 jit_solution(18142098531981148386)
XLA Ops:
  0.0 117.2 %shard_map.73 = bf16[1024,512]{1,0:T(8,128)(2,1)} custom-call(bf16[512,768]{1,0:T(8,128)(2,1)} %bitcast.5, bf16[768,512]{1,0:T(8,128)(2,1)} %bitcast.6, bf16[1,768,768]{2,1,0:T(8,128)(2,1)} %bitcast.4, bf16[2,128,128]{2,1,0:T(8,128)(2,1)} %piv_ref.1, s32[2,32]{1,0:T(2,128)} %bitcast.7, s32[32]{0:T(128)} %ord_ref.1, s32[2]{0:T(128)} %sep_ref.1), custom_call_target="tpu_custom_call" | custom-call | flops 6000000000 | bytes 5000000 | tf_op jit(solution)/shard_map/pallas_call | solution.py:489
  117.2 2.3 %copy.9 = bf16[1024,512]{1,0:T(8,128)(2,1)} copy(bf16[1024,512]{1,0:T(8,128)(2,1)} %shard_map.73) | data formatting | bytes 2097152

commit v6 on v5

--- a/solution.py
+++ b/solution.py
@@ -30,7 +30,7 @@
     nz = col_count // 2
     blocks = cols // NB
     per_half = half // NB
-    few = max(piece_rows // 16, 16)
+    few = max(piece_rows // 8, 16)
     layer = lax.axis_index("layer")
     core, xx = layer % 2, layer // 2
     ci = lax.axis_index("col")

time: 120 us -> 123 us (1.025)
  Pallas kernels: 117 us -> 120 us
    pallas_call x1, Pallas kernels: 117 us -> 120 us  [fused(): pl.pallas_call(functools.partial(fused_kernel, col_count), out_shape=jax....]
where the time goes in v6:
time: 123 us
  Pallas kernels  120 us (98%)
  local copies, waits for them, and re-layouts  2.26 us (2%)
    pallas_call x1, Pallas kernels, fused(): pl.pallas_call(functools.partial(fused_kernel, col_count), out_shape=jax....  120 us

profile of v6, /device:TPU:25, one launch (start us, length us, event | category | flops | bytes accessed | tf_op | source)
XLA Modules:
  0.0 122.7 jit_solution(6252453933337280596)
XLA Ops:
  0.0 120.4 %shard_map.73 = bf16[1024,512]{1,0:T(8,128)(2,1)} custom-call(bf16[512,768]{1,0:T(8,128)(2,1)} %bitcast.5, bf16[768,512]{1,0:T(8,128)(2,1)} %bitcast.6, bf16[1,768,768]{2,1,0:T(8,128)(2,1)} %bitcast.4, bf16[2,128,128]{2,1,0:T(8,128)(2,1)} %piv_ref.1, s32[2,32]{1,0:T(2,128)} %bitcast.7, s32[32]{0:T(128)} %ord_ref.1, s32[2]{0:T(128)} %sep_ref.1), custom_call_target="tpu_custom_call" | custom-call | flops 6000000000 | bytes 5000000 | tf_op jit(solution)/shard_map/pallas_call | solution.py:489
  120.4 2.3 %copy.9 = bf16[1024,512]{1,0:T(8,128)(2,1)} copy(bf16[1024,512]{1,0:T(8,128)(2,1)} %shard_map.73) | data formatting | bytes 2097152

commit v7 on v6

--- a/solution.py
+++ b/solution.py
@@ -30,7 +30,7 @@
     nz = col_count // 2
     blocks = cols // NB
     per_half = half // NB
-    few = max(piece_rows // 8, 16)
+    few = max(piece_rows // 32, 16)
     layer = lax.axis_index("layer")
     core, xx = layer % 2, layer // 2
     ci = lax.axis_index("col")
@@ -83,16 +83,19 @@
 
     pl.semaphore_wait(barrier, 3 + jnp.where(has_right, 1, 0) + jnp.where(has_left, 1, 0))
 
-    parts = 4
-    part = v0.shape[0] // parts
-    y_first, z_first = (0, 1), (2, 3)
-
-    def vpart(k):
-        return pl.ds(k * part, part)
+    parts = 2
+    part = v0.shape[0] // (2 * parts)
+
+    def vpart(k, line=y):
+        return pl.ds(pl.multiple_of((line * parts + k) * part, part), part)
 
     def v_y(k):
-        src = v0 if k in y_first else vbase
-        return copy(src.at[vpart(k)], vy.at[vpart(k)], yv_send.at[k], vy_recv.at[k], y_peer)
+        rows = vpart(k, 1 - y)
+        return copy(v0.at[rows], vy.at[rows], yv_send.at[k], vy_recv.at[k], y_peer)
+
+    def v_sum(k):
+        rows = vpart(k)
+        return copy(vbase.at[rows], vbase.at[rows], yv_send.at[parts + k], vy_recv.at[parts + k], y_peer)
 
     def v_right(k):
         return copy(vsr.at[vpart(k)], vr.at[vpart(k)], vr_send.at[k], vr_recv.at[k], right)
@@ -132,20 +135,8 @@
         pl.when(z < nz // 2)(functools.partial(add_left, k))
         pl.when(z >= nz // 2)(functools.partial(add_right, k))
 
-    for k in y_first:
+    for k in range(parts):
         v_y(k).start()
-    vsr[...] = v0[...]
-    vsl[...] = v0[...]
-
-    @pl.when(z == 0)
-    def _():
-        for k in z_first:
-            v_right(k).start()
-
-    @pl.when(z == nz - 1)
-    def _():
-        for k in z_first:
-            v_left(k).start()
 
     lbuf[piece(ci), :] = l_ref[...]
 
@@ -190,12 +181,7 @@
 
     s_acc[...] = jnp.zeros_like(s_acc)
 
-    @pl.when((z > 0) & (z < nz - 1))
-    def _():
-        for k in z_first:
-            near_way(k)
-
-    for k in y_first:
+    for k in range(parts):
         rows = vpart(k)
         v_y(k).wait_recv()
         summed = v0[rows, :] + vy[rows, :]
@@ -203,13 +189,11 @@
         vsr[rows, :] = summed
         vsl[rows, :] = summed
         near_way(k)
-    for k in z_first:
+    for k in range(parts):
         rows = vpart(k)
         far_way(k)
-        vbase[rows, :] = vsr[rows, :] + vsl[rows, :] - v0[rows, :]
-        v_y(k).start()
-    for k in y_first:
-        far_way(k)
+        vbase[rows, :] = vsr[rows, :] + vsl[rows, :] - vbase[rows, :]
+        v_sum(k).start()
 
     other = ci + 1 - 2 * y
     tail_over_y(other).wait_recv()
@@ -257,16 +241,10 @@
                 rounded[:, b * NB : (b + 1) * NB] * flag
             ).astype(BF16)
 
-    for k in z_first:
-        rows = vpart(k)
-        v_y(k).wait_recv()
-        v0[rows, :] = vbase[rows, :] + vy[rows, :]
-    for k in y_first:
-        rows = vpart(k)
-        v_y(k).wait_send()
-        v0[rows, :] = vsr[rows, :] + vsl[rows, :] - vbase[rows, :]
+    for k in range(parts):
+        v_sum(k).wait_recv()
     for s in range(supers):
-        solved = dot(d_ref[s], v0[s * node : (s + 1) * node, :])
+        solved = dot(d_ref[s], vbase[s * node : (s + 1) * node, :])
         rounded = solved.astype(BF16).astype(F32)
         for k in range(2):
             held = jnp.int32(0)
@@ -424,8 +402,8 @@
     over_x.wait_send()
     share.wait_send()
     for k in range(parts):
-        if k in z_first:
-            v_y(k).wait_send()
+        v_y(k).wait_send()
+        v_sum(k).wait_send()
 
         @pl.when(has_right)
         def _():

time: 123 us -> 115 us (0.935)
  the two profiles are of different devices: /device:TPU:25 before, /device:TPU:2 now
where the time goes in v7:
time: 115 us
  Pallas kernels  113 us (98%)
  local copies, waits for them, and re-layouts  2.26 us (2%)
    pallas_call x1, Pallas kernels, fused(): pl.pallas_call(functools.partial(fused_kernel, col_count), out_shape=jax....  113 us

profile of v7, /device:TPU:2, one launch (start us, length us, event | category | flops | bytes accessed | tf_op | source)
XLA Modules:
  0.0 114.9 jit_solution(3250116036884124645)
XLA Ops:
  0.0 112.6 %shard_map.73 = bf16[1024,512]{1,0:T(8,128)(2,1)} custom-call(bf16[512,768]{1,0:T(8,128)(2,1)} %bitcast.5, bf16[768,512]{1,0:T(8,128)(2,1)} %bitcast.6, bf16[1,768,768]{2,1,0:T(8,128)(2,1)} %bitcast.4, bf16[2,128,128]{2,1,0:T(8,128)(2,1)} %piv_ref.1, s32[2,32]{1,0:T(2,128)} %bitcast.7, s32[32]{0:T(128)} %ord_ref.1, s32[2]{0:T(128)} %sep_ref.1), custom_call_target="tpu_custom_call" | custom-call | flops 6000000000 | bytes 5000000 | tf_op jit(solution)/shard_map/pallas_call | solution.py:467
  112.6 2.3 %copy.9 = bf16[1024,512]{1,0:T(8,128)(2,1)} copy(bf16[1024,512]{1,0:T(8,128)(2,1)} %shard_map.73) | data formatting | bytes 2097152
